TPU v7x, 32 devices: a whole 2x2x4 slice. The times are simulated.
32 devices in a mesh: grp: 2 (over y), gx: 4 (over x, core), gy: 4 (over z).
Axes of the slice: x: 2, y: 2, z: 4, core: 2. Of those that a mesh axis runs over, the one named last changes fastest.
Arguments:
- hidden: bfloat16 [1088, 8, 3200], P('gy', 'grp', 'gx'), parts along dimension 1, may hold values from -6 to 6
- qkv: bfloat16 [1088, 8, 6144], P('gy', 'grp', 'gx'), parts along dimension 1, may hold values from -10 to 10
- w_qkv: bfloat16 [3200, 6144], P('gy', 'gx'), may hold values from -0.109375 to 0.109375
- w_out: bfloat16 [3200, 2048], P('gy', 'gx'), may hold values from -0.109375 to 0.109375
- grad_out: bfloat16 [1088, 8, 3200], P('gy', 'grp', 'gx'), parts along dimension 1, may hold values from -6 to 6
- lengths: int32 [8], P('grp'), parts along dimension 0, may hold values from 544 to 1088, as said below
Outputs:
- grad_hidden: bfloat16 [1088, 8, 3200], P('gy', 'grp', 'gx'), parts along dimension 1
- grad_w_qkv: float32 [6400, 6144], P(('grp', 'gy'), 'gx'), parts along dimension 0
- grad_w_out: float32 [6400, 2048], P(('grp', 'gy'), 'gx'), parts along dimension 0
There are 2 independent parts, one for each index of `grp`. A program takes and returns all parts, laid end to end along the dimension named above; an argument that names none is the same for every part. Nothing has to cross between parts.
Inputs may be any that keep to these rules, and one draw needn't show every extreme that they name: Keys at positions lengths[b] and beyond are masked for image b; exactly one image has all 1088 slots valid.
All inputs are finite; a program needn't handle non-finite values.
Results may differ from a plain program's by a relative error of at most 0.017.
Values may be sent and summed in bfloat16 or wider, within the bound.
A program may use at most 256 MiB of HBM per device.

v0:
```python
import math

import jax
import jax.numpy as jnp
from jax import lax
from jax.sharding import PartitionSpec as P

D = 3200
HEAD_DIM = 128


def contract_rows(left_rows, right_rows):
    return lax.dot_general(
        left_rows, right_rows, (((0,), (0,)), ((), ())), preferred_element_type=jnp.float32
    )


def softmax_totals(scores, valid_grid):
    masked = jnp.where(valid_grid, scores, -jnp.inf)
    row_max = jnp.max(masked, axis=3, keepdims=True)
    row_total = jnp.sum(
        jnp.where(valid_grid, jnp.exp(scores - row_max), 0.0), axis=3, keepdims=True
    )
    return row_max + jnp.log(row_total)


def shards(hidden, qkv, w_qkv, w_out, grad_out, lengths):
    seq_dev, image_count, column_count = qkv.shape
    heads_dev = column_count // (3 * HEAD_DIM)
    score_scale = 1.0 / math.sqrt(HEAD_DIM)
    row_count = seq_dev * image_count
    qkv_parts = qkv.reshape(seq_dev, image_count, heads_dev, 3, HEAD_DIM)
    query_rows = qkv_parts[:, :, :, 0]
    key_values = qkv_parts[:, :, :, 1:].reshape(seq_dev, image_count, heads_dev * 2 * HEAD_DIM)
    grad_full, hidden_full = (
        lax.all_gather(grad_out, "gx", axis=2, tiled=True),
        lax.all_gather(hidden, "gx", axis=2, tiled=True),
    )
    w_qkv_full, w_out_full, kv_full = (
        lax.all_gather(w_qkv, "gy", axis=0, tiled=True),
        lax.all_gather(w_out, "gy", axis=0, tiled=True),
        lax.all_gather(key_values, "gy", axis=0, tiled=True),
    )
    grad_rows = grad_full.reshape(row_count, D)
    grad_attn = jnp.dot(grad_rows, w_out_full, preferred_element_type=jnp.float32).astype(
        jnp.bfloat16
    )
    grad_attn = grad_attn.reshape(seq_dev, image_count, heads_dev, HEAD_DIM)
    seq_total = kv_full.shape[0]
    kv_parts = kv_full.reshape(seq_total, image_count, heads_dev, 2, HEAD_DIM)
    key_all = kv_parts[:, :, :, 0]
    value_all = kv_parts[:, :, :, 1]
    valid_all = (jnp.arange(seq_total)[None, :] < lengths[:, None])[:, None, None, :]
    scores = (
        jnp.einsum("sbhe,tbhe->bhst", query_rows, key_all, preferred_element_type=jnp.float32)
        * score_scale
    )
    log_total = softmax_totals(scores, valid_all)
    probs_full = jnp.where(valid_all, jnp.exp(scores - log_total), 0.0)
    probs_low = probs_full.astype(jnp.bfloat16)
    attn_out = jnp.einsum(
        "bhst,tbhe->sbhe", probs_low, value_all, preferred_element_type=jnp.float32
    ).astype(jnp.bfloat16)
    row_dots = jnp.sum(grad_attn.astype(jnp.float32) * attn_out.astype(jnp.float32), axis=3)
    dots_grid = row_dots.transpose(1, 2, 0)[..., None]
    grad_prob = jnp.einsum(
        "sbhe,tbhe->bhst", grad_attn, value_all, preferred_element_type=jnp.float32
    )
    grad_score = (probs_full * (grad_prob - dots_grid) * score_scale).astype(jnp.bfloat16)
    grad_q = jnp.einsum(
        "bhst,tbhe->sbhe", grad_score, key_all, preferred_element_type=jnp.float32
    ).astype(jnp.bfloat16)
    key_terms = jnp.einsum(
        "bhst,sbhe->tbhe", grad_score, query_rows, preferred_element_type=jnp.float32
    )
    value_terms = jnp.einsum(
        "bhst,sbhe->tbhe", probs_low, grad_attn, preferred_element_type=jnp.float32
    )
    kv_terms = jnp.stack([key_terms, value_terms], axis=3).reshape(
        seq_total, image_count, heads_dev * 2 * HEAD_DIM
    )
    summed = lax.psum_scatter(kv_terms, "gy", scatter_dimension=0, tiled=True)
    grad_kv = summed.astype(jnp.bfloat16).reshape(seq_dev, image_count, heads_dev, 2, HEAD_DIM)
    grad_qkv = jnp.concatenate([grad_q[:, :, :, None], grad_kv], axis=3).reshape(
        seq_dev, image_count, column_count
    )
    grad_qkv_rows = grad_qkv.reshape(row_count, column_count)
    hidden_terms = lax.dot_general(
        grad_qkv_rows, w_qkv_full, (((1,), (1,)), ((), ())), preferred_element_type=jnp.float32
    )
    grad_hidden = lax.psum_scatter(
        hidden_terms.reshape(seq_dev, image_count, D), "gx", scatter_dimension=2, tiled=True
    ).astype(jnp.bfloat16)
    attn_rows = attn_out.reshape(row_count, heads_dev * HEAD_DIM)
    out_terms = contract_rows(grad_rows, attn_rows)
    qkv_terms = contract_rows(hidden_full.reshape(row_count, D), grad_qkv_rows)
    grad_w_qkv, grad_w_out = (
        lax.psum_scatter(qkv_terms, "gy", scatter_dimension=0, tiled=True),
        lax.psum_scatter(out_terms, "gy", scatter_dimension=0, tiled=True),
    )
    return (grad_hidden, grad_w_qkv, grad_w_out)


def solution(mesh):
    placed = (
        P("gy", "grp", "gx"),
        P("gy", "grp", "gx"),
        P("gy", "gx"),
        P("gy", "gx"),
        P("gy", "grp", "gx"),
        P("grp"),
    )
    return jax.shard_map(
        shards,
        mesh=mesh,
        in_specs=placed,
        out_specs=(P("gy", "grp", "gx"), P(("grp", "gy"), "gx"), P(("grp", "gy"), "gx")),
        check_vma=False,
    )
```

profile of v0, /device:TPU:0, one launch (start us, length us, event | category | flops | bytes accessed | tf_op | source)
XLA Modules:
  0.0 1725.9 jit_solution(7326093041001458450)
XLA Ops:
  7.2 0.0 all-gather.8.cloned.1.call-start
  7.2 6.2 copy.54
  13.4 0.0 all-gather.8.cloned.1.call-update
  13.5 0.0 all-gather.10.cloned.1.call-start
  13.5 0.7 all-gather.10.cloned.1.call-update
  14.2 0.0 all-gather.6.cloned.1.call-start
  14.3 2.6 copy.50
  16.8 4.6 reshape.63
  21.5 5.3 slice.17
  26.7 2.8 reshape.64
  29.6 0.0 all-gather.12.cloned.1.call-start
  29.7 0.5 all-gather.12.cloned.1.call-update
  30.2 0.0 all-gather.14.cloned.1.call-start
  30.2 6.2 copy.64
  36.5 0.0 reduce-scatter.10.cloned.1.call-start
  36.6 3.8 slice.16
  40.4 0.1 iota_compare_fusion
  40.5 0.7 dynamic-slice
  41.9 40.9 %all-gather.8.cloned.1.call-done = bf16[272,4,3200]{0,1,2:T(4,128)(2,1)} async-done(((bf16[272,4,800]{0,1,2:T(4,128)(2,1)}), bf16[272,4,3200]{0,1,2:T(4,128)(2,1)}) %all-gather.8.cloned.1.call-update) | async-done | bytes 6963216 | tf_op jit(solution)/shard_map/all_gather | solution.py:36
  82.8 20.1 %copy.55 = bf16[272,4,3200]{2,1,0:T(4,128)(2,1)} copy(bf16[272,4,3200]{0,1,2:T(4,128)(2,1)} %all-gather.8.cloned.1.call-done) | data formatting | bytes 13926400 | tf_op jit(solution)/shard_map/all_gather | solution.py:36
  102.9 11.6 reshape.66
  114.5 35.6 %all-gather.10.cloned.1.call-done = bf16[3200,512]{1,0:T(8,128)(2,1)} async-done(((bf16[800,512]{1,0:T(8,128)(2,1)}), bf16[3200,512]{1,0:T(8,128)(2,1)}) %all-gather.10.cloned.1.call-update) | async-done | bytes 3276816 | tf_op jit(solution)/shard_map/all_gather | solution.py:41
  150.1 8.9 convolution_convert_fusion
  159.0 3.3 reshape.67
  162.2 146.3 %all-gather.6.cloned.1.call-done = bf16[1088,4,1024]{2,0,1:T(8,128)(2,1)} async-done(((bf16[272,4,1024]{2,0,1:T(8,128)(2,1)}), bf16[1088,4,1024]{2,0,1:T(8,128)(2,1)}) %all-gather.6.cloned.1.call-update) | async-done | bytes 8912912 | tf_op jit(solution)/shard_map/all_gather | solution.py:42
  308.5 12.3 copy.52
  320.8 12.8 select_reduce_fusion.1
  333.6 9.2 select_reduce_fusion
  342.9 9.9 multiply_reduce_fusion
  352.7 13.0 convolution_bitcast_fusion.2
  365.7 14.7 multiply_convert_fusion
  380.4 11.3 convolution_bitcast_fusion.3
  391.8 11.9 pad_maximum_fusion
  403.7 18.4 %copy.60 = f32[1088,4,4,2,128]{0,4,3,2,1:T(8,128)} copy(f32[1088,4,4,2,128]{4,0,2,1,3:T(8,128)} %pad_maximum_fusion) | data formatting | bytes 35651584 | tf_op jit(solution)/shard_map/stack | solution.py:79
  422.2 22.6 %copy.61 = f32[1088,4,1024]{2,1,0:T(4,128)} copy(f32[1088,4,1024]{0,2,1:T(8,128)} %bitcast.80) | data formatting | bytes 35651584 | tf_op jit(solution)/shard_map/reshape | solution.py:79
  444.8 620.4 %all-reduce.2 = bf16[1088,4,1024]{2,1,0:T(4,128)(2,1)} all-reduce(f32[1088,4,1024]{2,1,0:T(4,128)} %copy.61), channel_id=2, replica_groups=mesh['grp'=2,'gx'=4,'gy'=4] {'gy'}, use_global_device_ids=true, to_apply=%region_3.4.clone | all-reduce | flops 4456448 | bytes 26738688
  1065.2 3.8 dynamic-slice_convert_fusion
  1069.0 5.4 reshape.69
  1074.4 7.9 fusion.9
  1082.3 1.7 copy.62
  1084.0 7.0 pad_maximum_fusion.1
  1091.0 8.6 reshape.73
  1099.7 0.0 all-gather.12.cloned.1.call-done
  1099.7 18.3 %fusion.1 = f32[272,4,3200]{2,0,1:T(8,128)} fusion(bf16[3200,1536]{1,0:T(8,128)(2,1)} %all-gather.12.cloned.1.call-done, bf16[272,4,1536]{2,1,0:T(4,128)(2,1)S(1)} %reshape.73), kind=kOutput, calls=%fused_computation.7 | convolution fusion | flops 10695475200 | bytes 27099136 | tf_op jit(solution)/shard_map/dot_general | solution.py:88
  1118.0 19.7 %copy.71 = f32[272,4,3200]{0,1,2:T(4,128)} copy(f32[272,4,3200]{2,0,1:T(8,128)} %fusion.1) | data formatting | bytes 27852800
  1137.7 20.6 %reshape.74 = f32[3200,1088]{1,0:T(8,128)} reshape(f32[3200,4,272]{2,1,0:T(4,128)} %bitcast.79) | data formatting | bytes 27852800
  1158.3 0.0 reduce-scatter.14.cloned.1.call-start
  1158.4 1.2 copy-done.3
  1159.6 0.4 copy.66
  1160.0 9.9 convolution_bitcast_fusion.1
  1169.9 9.0 copy.75
  1179.0 0.0 reduce-scatter.12.cloned.1.call-start
  1179.0 0.0 all-gather.14.cloned.1.call-done
  1179.1 20.2 %copy.65 = bf16[272,4,3200]{2,1,0:T(4,128)(2,1)} copy(bf16[272,4,3200]{0,1,2:T(4,128)(2,1)} %all-gather.14.cloned.1.call-done) | data formatting | bytes 13926400 | tf_op jit(solution)/shard_map/all_gather | solution.py:37
  1199.2 11.7 reshape.70
  1211.0 7.9 reshape_reshape.3
  1219.0 19.7 %convolution_bitcast_fusion = f32[3200,1536]{0,1:T(8,128)} fusion(bf16[1088,1536]{1,0:T(8,128)(2,1)S(1)} %reshape_reshape.3, bf16[1088,3200]{1,0:T(8,128)(2,1)} %reshape.70), kind=kOutput, calls=%fused_computation.5 | convolution fusion | flops 10695475200 | bytes 29966336 | tf_op jit(solution)/shard_map/dot_general | solution.py:13
  1238.7 20.2 %copy.73 = f32[3200,1536]{1,0:T(8,128)} copy(f32[3200,1536]{0,1:T(8,128)} %convolution_bitcast_fusion) | data formatting | bytes 39321600
  1258.9 12.0 reduce-scatter.10.cloned.1.call-done
  1270.9 4.0 reshape.75
  1275.0 4.5 copy.72
  1279.5 4.1 copy.67
  1283.6 105.2 %reduce-scatter.14.cloned.1.call-done = f32[800,512]{1,0:T(8,128)} async-done(((f32[3200,512]{1,0:T(8,128)}), f32[800,512]{1,0:T(8,128)}) %reduce-scatter.14.cloned.1.call-update) | async-done | bytes 1638416
  1388.9 329.8 %reduce-scatter.12.cloned.1.call-done = f32[800,1536]{1,0:T(8,128)} async-done(((f32[3200,1536]{1,0:T(8,128)}), f32[800,1536]{1,0:T(8,128)}) %reduce-scatter.12.cloned.1.call-update) | async-done | bytes 4915216
  (24 shorter events, 0.1 us)
Async XLA Ops:
  7.2 75.6 %all-gather.8.cloned.1.call-start = ((), (), s32[]{:S(2)}) async-start(), calls=%async_computation.4 | async-start | bytes 12288000 | tf_op jit(solution)/shard_map/all_gather | solution.py:36
  13.5 136.6 %all-gather.10.cloned.1.call-start = ((), (), s32[]{:S(2)}) async-start(), calls=%async_computation.5 | async-start | bytes 4096000 | tf_op jit(solution)/shard_map/all_gather | solution.py:41
  14.2 294.3 %all-gather.6.cloned.1.call-start = ((), (), s32[]{:S(2)}) async-start(), calls=%async_computation.3 | async-start | bytes 11141120 | tf_op jit(solution)/shard_map/all_gather | solution.py:42
  29.6 10.8 copy-start.4
  29.6 10.9 copy-start.5
  29.6 1070.1 %all-gather.12.cloned.1.call-start = ((), (), s32[]{:S(2)}) async-start(), calls=%async_computation.6 | async-start | bytes 12288000 | tf_op jit(solution)/shard_map/all_gather | solution.py:40
  30.2 1148.9 %all-gather.14.cloned.1.call-start = ((), (), s32[]{:S(2)}) async-start(), calls=%async_computation.7 | async-start | bytes 12288000 | tf_op jit(solution)/shard_map/all_gather | solution.py:37
  36.5 1234.4 %reduce-scatter.10.cloned.1.call-start = ((), (), s32[]{:S(2)}) async-start(), calls=%async_computation.8 | async-start | bytes 18432000
  40.4 280.4 %copy-start = (bf16[272,4,4,1,128]{4,3,2,0,1:T(2,128)(2,1)}, bf16[272,4,4,1,128]{4,3,2,0,1:T(2,128)(2,1)S(1)}, u32[]{:S(2)}) copy-start(bf16[272,4,4,1,128]{4,3,2,0,1:T(2,128)(2,1)S(1)} %slice.16) | copy-start | bytes 3342340
  320.8 22.0 %slice-start = ((s8[9437184]{0:T(1024)(128)(4,1)}), s8[4194304]{0:T(1024)(128)(4,1)S(1)}, s32[]{:S(2)}) async-start(s8[9437184]{0:T(1024)(128)(4,1)} %bitcast.84), calls=%async_computation.11 | async-start | bytes 8388608
  320.8 22.1 %slice-start.1 = ((s8[9437184]{0:T(1024)(128)(4,1)}), s8[4194304]{0:T(1024)(128)(4,1)S(1)}, s32[]{:S(2)}) async-start(s8[9437184]{0:T(1024)(128)(4,1)} %bitcast.84), calls=%async_computation.12 | async-start | bytes 8388608
  333.6 9.2 slice-start.2
  333.6 9.3 copy-start.2
  365.7 14.7 copy-start.1
  1158.3 1.2 copy-start.3
  1158.3 230.5 %reduce-scatter.14.cloned.1.call-start = ((), (), s32[]{:S(2)}) async-start(), calls=%async_computation.10 | async-start | bytes 8192000
  1179.0 539.7 %reduce-scatter.12.cloned.1.call-start = ((), (), s32[]{:S(2)}) async-start(), calls=%async_computation.9 | async-start | bytes 24576000
Sparse Core Ops, SparseCore 0:
  13.6 69.1 all-gather.7
  84.3 65.6 all-gather.9
  151.6 156.8 all-gather.5
  309.9 201.5 all-gather.11
  513.0 64.4 all-gather.13
  1158.5 112.4 reduce-scatter.9
  1273.8 115.0 reduce-scatter.13
  1391.8 326.7 reduce-scatter.11
where the time goes:
time: 1740 us; the launch traced here: 1730 us
  waiting for transfers between devices  671 us (39%)
  blocking collectives  620 us (36%)
  local copies, waits for them, and re-layouts  264 us (15%)
  matrix products  127 us (7%)
  other arithmetic  28.2 us (2%)
    unnamed x1, blocking collectives  620 us
    unnamed x11, waiting for transfers between devices  448 us
    all_gather x1, waiting for transfers between devices, shards(): lax.all_gather(key_values, 'gy', axis=0, tiled=True)  146 us
    unnamed x29, local copies, waits for them, and re-layouts  99.2 us
    all_gather x1, waiting for transfers between devices, shards(): lax.all_gather(grad_out, 'gx', axis=2, tiled=True)  40.9 us
    all_gather x1, waiting for transfers between devices, shards(): lax.all_gather(w_out, 'gy', axis=0, tiled=True)  35.6 us
  transfers between devices with their start and end apart: 8, of which 6 were waited for; matrix products, arithmetic and copies ran while one was open for 24% of the time, Pallas kernels for 0%

commit v1 on v0

--- a/solution.py
+++ b/solution.py
@@ -1,8 +1,11 @@
+import functools
 import math
 
 import jax
 import jax.numpy as jnp
 from jax import lax
+from jax.experimental import pallas as pl
+from jax.experimental.pallas import tpu as pltpu
 from jax.sharding import PartitionSpec as P
 
 D = 3200
@@ -101,7 +104,169 @@
     return (grad_hidden, grad_w_qkv, grad_w_out)
 
 
+def dot(left, right, dims):
+    return lax.dot_general(left, right, ((dims[0], dims[1]), ((), ())), preferred_element_type=jnp.float32)
+
+
+def head_kernel(block, length_ref, qkv_ref, grad_ref, attn_ref, dqkv_ref, key_sum, value_sum):
+    seq = qkv_ref.shape[0]
+    score_scale = 1.0 / math.sqrt(HEAD_DIM)
+    length = length_ref[0]
+    key_sum[...] = jnp.zeros_like(key_sum)
+    value_sum[...] = jnp.zeros_like(value_sum)
+
+    @pl.loop(0, seq // block)
+    def _(step):
+        rows = pl.ds(pl.multiple_of(step * block, block), block)
+        q = qkv_ref[rows, 0:HEAD_DIM]
+        k = qkv_ref[:, HEAD_DIM : 2 * HEAD_DIM]
+        v = qkv_ref[:, 2 * HEAD_DIM :]
+        g = grad_ref[rows, :]
+        valid = lax.broadcasted_iota(jnp.int32, (1, seq), 1) < length
+        scores = dot(q, k, ((1,), (1,))) * score_scale
+        masked = jnp.where(valid, scores, -jnp.inf)
+        row_max = jnp.max(masked, axis=1, keepdims=True)
+        terms = jnp.exp(masked - row_max)
+        probs = terms * (1.0 / jnp.sum(terms, axis=1, keepdims=True))
+        probs_low = probs.astype(jnp.bfloat16)
+        attn = dot(probs_low, v, ((1,), (0,))).astype(jnp.bfloat16)
+        attn_ref[rows, :] = attn
+        row_dots = jnp.sum(g.astype(jnp.float32) * attn.astype(jnp.float32), axis=1, keepdims=True)
+        grad_prob = dot(g, v, ((1,), (1,)))
+        grad_score = (probs * ((grad_prob - row_dots) * score_scale)).astype(jnp.bfloat16)
+        dqkv_ref[rows, 0:HEAD_DIM] = dot(grad_score, k, ((1,), (0,))).astype(jnp.bfloat16)
+        key_sum[...] += dot(grad_score, q, ((0,), (0,)))
+        value_sum[...] += dot(probs_low, g, ((0,), (0,)))
+
+    dqkv_ref[:, HEAD_DIM : 2 * HEAD_DIM] = key_sum[...].astype(jnp.bfloat16)
+    dqkv_ref[:, 2 * HEAD_DIM :] = value_sum[...].astype(jnp.bfloat16)
+
+
+def attention_backward(length, qkv, grad_attn):
+    seq = qkv.shape[0]
+    heads = qkv.shape[1] // (3 * HEAD_DIM)
+    block = 272 if seq % 272 == 0 else seq
+    return pl.pallas_call(
+        functools.partial(head_kernel, block),
+        grid=(heads,),
+        in_specs=[
+            pl.BlockSpec(memory_space=pltpu.SMEM),
+            pl.BlockSpec((seq, 3 * HEAD_DIM), lambda h: (0, h)),
+            pl.BlockSpec((seq, HEAD_DIM), lambda h: (0, h)),
+        ],
+        out_specs=[
+            pl.BlockSpec((seq, HEAD_DIM), lambda h: (0, h)),
+            pl.BlockSpec((seq, 3 * HEAD_DIM), lambda h: (0, h)),
+        ],
+        out_shape=[
+            jax.ShapeDtypeStruct((seq, heads * HEAD_DIM), jnp.bfloat16),
+            jax.ShapeDtypeStruct((seq, heads * 3 * HEAD_DIM), jnp.bfloat16),
+        ],
+        scratch_shapes=[
+            pltpu.VMEM((seq, HEAD_DIM), jnp.float32),
+            pltpu.VMEM((seq, HEAD_DIM), jnp.float32),
+        ],
+        compiler_params=pltpu.CompilerParams(vmem_limit_bytes=40 * 2**20),
+        cost_estimate=pl.CostEstimate(
+            flops=14 * heads * seq * seq * HEAD_DIM,
+            bytes_accessed=16 * heads * seq * HEAD_DIM,
+            transcendentals=heads * seq * seq,
+        ),
+    )(length, qkv, grad_attn)
+
+
+def by_image(rows):
+    swapped = lax.all_to_all(rows.transpose(1, 0, 2), "gy", 0, 0)
+    return swapped.reshape(-1, rows.shape[2])
+
+
+def weight_rows(weight):
+    half = weight.shape[0] // 2
+    group, me = lax.axis_index("grp"), lax.axis_index("gy")
+    share = lax.dynamic_slice_in_dim(weight, group * half, half, 0)
+    mine = lax.all_gather(share, "gy")
+    full = jnp.zeros((4, 2) + share.shape, weight.dtype)
+    full = lax.dynamic_update_slice(full, weight.reshape((1, 2) + share.shape), (me, 0, 0, 0))
+    for bits in (1, 2, 3):
+        part = lax.dynamic_slice_in_dim(mine, me ^ bits, 1, 0)
+        other = lax.ppermute(part, "grp", [(0, 1), (1, 0)])
+        full = lax.dynamic_update_slice(full, part[None], (me ^ bits, group, 0, 0))
+        full = lax.dynamic_update_slice(full, other[None], (me ^ bits, 1 - group, 0, 0))
+    return full.reshape((4,) + weight.shape)
+
+
+def spread_images(rows):
+    me = lax.axis_index("gy")
+    blocks = rows.transpose(1, 0, 2)
+    full = jnp.zeros(blocks.shape, blocks.dtype)
+    for bits in range(4):
+        part = lax.dynamic_index_in_dim(blocks, me ^ bits, 0, keepdims=False)
+        if bits:
+            part = lax.ppermute(part, "gy", [(i, i ^ bits) for i in range(4)])
+        full = lax.dynamic_update_index_in_dim(full, part, me ^ bits, 0)
+    return full.reshape(-1, rows.shape[2])
+
+
+def flip(value, bits):
+    return lax.ppermute(value, "gx", [(i, i ^ bits) for i in range(4)])
+
+
+def feature_blocks(own):
+    across = flip(own, 2)
+    beside = flip(own, 1)
+    corner = flip(across, 1)
+    me = lax.axis_index("gx")
+    full = jnp.zeros((4,) + own.shape, own.dtype)
+    for bits, part in enumerate((own, beside, across, corner)):
+        full = lax.dynamic_update_index_in_dim(full, part, me ^ bits, 0)
+    return full
+
+
+def sum_features(terms):
+    me = lax.axis_index("gx")
+
+    def block(bits):
+        return lax.dynamic_index_in_dim(terms, me ^ bits, 0, keepdims=False)
+
+    far = block(2).astype(jnp.float32) + flip(block(3), 1).astype(jnp.float32)
+    near = block(0).astype(jnp.float32) + flip(block(1), 1).astype(jnp.float32)
+    return (near + flip(far.astype(jnp.bfloat16), 2).astype(jnp.float32)).astype(jnp.bfloat16)
+
+
+def image_shards(gy_count, hidden, qkv, w_qkv, w_out, grad_out, lengths):
+    image = lax.axis_index("gy")
+    length = lax.dynamic_slice(lengths, (image,), (1,))
+    seq_dev = qkv.shape[0]
+    w_out_full = weight_rows(w_out)
+    grad_own = by_image(grad_out)
+    grad_rows = feature_blocks(grad_own)
+    qkv, grad_own = lax.optimization_barrier((qkv, grad_own))
+    qkv_rows = spread_images(qkv)
+    hidden, qkv_rows = lax.optimization_barrier((hidden, qkv_rows))
+    w_qkv, grad_own = lax.optimization_barrier((w_qkv, grad_own))
+    w_qkv_full = weight_rows(w_qkv)
+    hidden_rows = feature_blocks(spread_images(hidden))
+    w_qkv_full, hidden_rows = lax.optimization_barrier((w_qkv_full, hidden_rows))
+    grad_attn = jnp.einsum(
+        "ird,idc->rc", grad_rows, w_out_full, preferred_element_type=jnp.float32
+    ).astype(jnp.bfloat16)
+    attn_out, grad_qkv = attention_backward(length, qkv_rows, grad_attn)
+    out_terms = jnp.einsum("ird,rc->idc", grad_rows, attn_out, preferred_element_type=jnp.float32)
+    grad_w_out = lax.psum_scatter(out_terms.astype(jnp.bfloat16), "gy")
+    qkv_terms = jnp.einsum("ird,rc->idc", hidden_rows, grad_qkv, preferred_element_type=jnp.float32)
+    grad_w_qkv = lax.psum_scatter(qkv_terms.astype(jnp.bfloat16), "gy")
+    hidden_terms = jnp.einsum("rc,idc->ird", grad_qkv, w_qkv_full, preferred_element_type=jnp.float32)
+    grad_hidden = sum_features(hidden_terms.astype(jnp.bfloat16))
+    grad_hidden = grad_hidden.reshape(gy_count, seq_dev, -1)
+    grad_hidden = lax.all_to_all(grad_hidden, "gy", 0, 0).transpose(1, 0, 2)
+    return (grad_hidden, grad_w_qkv.astype(jnp.float32), grad_w_out.astype(jnp.float32))
+
+
 def solution(mesh):
+    gx_count, gy_count = mesh.shape["gx"], mesh.shape["gy"]
+    images = 8 // mesh.shape["grp"]
+    split_images = images == gy_count and gx_count == gy_count == 4 and mesh.shape["grp"] == 2
+    body = functools.partial(image_shards, gy_count) if split_images else shards
     placed = (
         P("gy", "grp", "gx"),
         P("gy", "grp", "gx"),
@@ -111,7 +276,7 @@
         P("grp"),
     )
     return jax.shard_map(
-        shards,
+        body,
         mesh=mesh,
         in_specs=placed,
         out_specs=(P("gy", "grp", "gx"), P(("grp", "gy"), "gx"), P(("grp", "gy"), "gx")),

time: 1740 us -> 714 us (0.41)
  blocking collectives: 620 us -> 0 us
  waiting for transfers between devices: 671 us -> 431 us
  local copies, waits for them, and re-layouts: 264 us -> 94.8 us
  matrix products: 127 us -> 43.4 us
  starting transfers between devices: 0.32 us -> 80.8 us
  Pallas kernels: 0 us -> 33.6 us
  other arithmetic: 28.2 us -> 8.37 us
    unnamed x1 -> x0, blocking collectives: 620 us -> none
    unnamed x11 -> x4, waiting for transfers between devices: 448 us -> 0.07 us
    ppermute x0 -> x21, waiting for transfers between devices: none -> 251 us  [the longest x6 117 us: spread_images(): part = lax.ppermute(part, 'gy', [(i, i ^ bits) for i in range(4)])]
    all_gather x5 -> x2, waiting for transfers between devices: 223 us -> 53.4 us  [weight_rows(): mine = lax.all_gather(share, 'gy')]
    all_to_all x0 -> x2, waiting for transfers between devices: none -> 93.8 us  [the longest x1 93.8 us: image_shards(): grad_hidden = lax.all_to_all(grad_hidden, 'gy', 0, 0).transpose(1, 0, 2)]
    unnamed x29 -> x40, local copies, waits for them, and re-layouts: 99.2 us -> 11.6 us
    dot_general x10 -> x4, matrix products: 127 us -> 43.4 us  [the longest x1 15.6 us: image_shards(): jnp.einsum('rc,idc->ird', grad_qkv, w_qkv_full, preferred_element_type=jn...]
    ppermute x0 -> x21, starting transfers between devices: none -> 62.1 us  [the longest x6 49.4 us: spread_images(): part = lax.ppermute(part, 'gy', [(i, i ^ bits) for i in range(4)])]
  transfers between devices with their start and end apart: 8 -> 27, of which waited for: 6 -> 15; matrix products, arithmetic and copies ran while one was open for 24% -> 19% of each run, Pallas kernels for 0% -> 5%
where the time goes in v1:
time: 714 us; the launch traced here: 706 us
  waiting for transfers between devices  431 us (60%)
  local copies, waits for them, and re-layouts  94.8 us (13%)
  starting transfers between devices  80.8 us (11%)
  matrix products  43.4 us (6%)
  Pallas kernels  33.6 us (5%)
  between operations  14.1 us (2%)
  other arithmetic  8.37 us (1%)
    ppermute x6, waiting for transfers between devices, spread_images(): part = lax.ppermute(part, 'gy', [(i, i ^ bits) for i in range(4)])  117 us
    all_to_all x1, waiting for transfers between devices, image_shards(): grad_hidden = lax.all_to_all(grad_hidden, 'gy', 0, 0).transpose(1, 0, 2)  93.8 us
    ppermute x6, waiting for transfers between devices, weight_rows(): other = lax.ppermute(part, 'grp', [(0, 1), (1, 0)])  68.6 us
    ppermute x9, waiting for transfers between devices, flip(): return lax.ppermute(value, 'gx', [(i, i ^ bits) for i in range(4)])  65 us
    all_gather x2, waiting for transfers between devices, weight_rows(): mine = lax.all_gather(share, 'gy')  53.4 us
    ppermute x6, starting transfers between devices, spread_images(): part = lax.ppermute(part, 'gy', [(i, i ^ bits) for i in range(4)])  49.4 us
    pallas_call x1, Pallas kernels, attention_backward(): pl.pallas_call(functools.partial(head_kernel, block), grid=(heads,), in_s...  33.6 us
    reduce_scatter x1, waiting for transfers between devices, image_shards(): grad_w_qkv = lax.psum_scatter(qkv_terms.astype(jnp.bfloat16), 'gy')  33.5 us
  transfers between devices with their start and end apart: 27, of which 15 were waited for; matrix products, arithmetic and copies ran while one was open for 19% of the time, Pallas kernels for 5%

profile of v1, /device:TPU:0, one launch (start us, length us, event | category | flops | bytes accessed | tf_op | source)
XLA Modules:
  0.0 706.5 jit_solution(16790702245954327671)
XLA Ops:
  7.2 1.8 constant_dynamic-slice_fusion.3
  9.1 3.0 copy.48
  12.1 6.4 all-to-all-start
  18.5 2.5 constant_dynamic-slice_fusion.7
  22.2 1.7 copy-done.11
  23.9 4.6 broadcast_in_dim.95
  28.6 1.6 constant_dynamic-update-slice_fusion.3
  30.2 53.4 %all-gather.7.cloned.1.call-done = bf16[1600,512]{1,0:T(8,128)(2,1)} async-done(((bf16[400,512]{1,0:T(8,128)(2,1)}), bf16[1600,512]{1,0:T(8,128)(2,1)}) %all-gather.7.cloned.1.call-update) | async-done | bytes 1638416 | tf_op jit(solution)/shard_map/all_gather | solution.py:187
  83.6 2.3 constant_dynamic-slice_fusion
  85.9 1.5 collective-permute-start.15
  87.9 1.5 collective-permute-start.17
  89.5 1.8 bitcast_dynamic-update-slice_fusion.25
  91.2 3.6 copy.31
  94.8 1.5 dynamic-slice_bitcast_fusion.2
  96.7 4.1 copy.43
  100.8 2.7 collective-permute-start.4
  103.5 3.9 copy.42
  110.1 1.7 collective-permute-start.5
  111.8 2.9 bitcast_dynamic-update-slice_fusion.24
  115.5 53.9 %collective-permute-done.3 = bf16[272,1536]{1,0:T(8,128)(2,1)} collective-permute-done((bf16[272,1536]{1,0:T(8,128)(2,1)}, bf16[272,1536]{1,0:T(8,128)(2,1)}, u32[]{:S(2)}, u32[]{:S(2)}) %collective-permute-start.3) | collective-permute-done | bytes 835616 | tf_op jit(solution)/shard_map/ppermute | solution.py:205
  169.4 1.2 bitcast_dynamic-update-slice_fusion.14
  170.6 16.8 %collective-permute-done.4 = bf16[272,1536]{1,0:T(8,128)(2,1)} collective-permute-done((bf16[272,1536]{1,0:T(8,128)(2,1)}, bf16[272,1536]{1,0:T(8,128)(2,1)}, u32[]{:S(2)}, u32[]{:S(2)}) %collective-permute-start.4) | collective-permute-done | bytes 835616 | tf_op jit(solution)/shard_map/ppermute | solution.py:205
  187.4 1.4 collective-permute-start.13
  188.8 1.2 bitcast_dynamic-update-slice_fusion.13
  190.0 16.8 %collective-permute-done.5 = bf16[272,1536]{1,0:T(8,128)(2,1)S(1)} collective-permute-done((bf16[272,1536]{1,0:T(8,128)(2,1)S(1)}, bf16[272,1536]{1,0:T(8,128)(2,1)S(1)}, u32[]{:S(2)}, u32[]{:S(2)}) %collective-permute-start.5) | collective-permute-done | bytes 835616 | tf_op jit(solution)/shard_map/ppermute | solution.py:205
  207.3 42.4 %collective-permute-start.6 = (bf16[272,800]{1,0:T(8,128)(2,1)S(1)}, bf16[272,800]{1,0:T(8,128)(2,1)S(1)}, u32[]{:S(2)}, u32[]{:S(2)}) collective-permute-start(bf16[272,800]{1,0:T(8,128)(2,1)S(1)} %get-tuple-element.33), channel_id=1, source_target_pairs={{0,1},{1,0},{2,3},{3,2},{4,5},{5,4},{6,7},{7,6},{8,9},{9,8},{10,11... | collective-permute-start | bytes 1305608 | tf_op jit(solution)/shard_map/ppermute | solution.py:205
  249.8 1.8 bitcast_dynamic-update-slice_fusion.22
  252.4 1.4 broadcast_in_dim.102
  254.6 12.7 %collective-permute-done.6 = bf16[272,800]{1,0:T(8,128)(2,1)S(1)} collective-permute-done((bf16[272,800]{1,0:T(8,128)(2,1)S(1)}, bf16[272,800]{1,0:T(8,128)(2,1)S(1)}, u32[]{:S(2)}, u32[]{:S(2)}) %collective-permute-start.6) | collective-permute-done | bytes 435232 | tf_op jit(solution)/shard_map/ppermute | solution.py:205
  267.3 2.6 collective-permute-start.8
  270.7 16.7 %collective-permute-done.7 = bf16[272,800]{1,0:T(8,128)(2,1)S(1)} collective-permute-done((bf16[272,800]{1,0:T(8,128)(2,1)S(1)}, bf16[272,800]{1,0:T(8,128)(2,1)S(1)}, u32[]{:S(2)}, u32[]{:S(2)}) %collective-permute-start.7) | collective-permute-done | bytes 435232 | tf_op jit(solution)/shard_map/ppermute | solution.py:205
  289.1 3.9 copy.40
  293.0 1.5 collective-permute-start.10
  294.5 1.8 bitcast_dynamic-update-slice_fusion.20
  296.8 3.9 copy.39
  302.5 4.3 bitcast_dynamic-update-slice_fusion.2
  306.8 3.0 bitcast_dynamic-update-slice_fusion.1
  309.9 20.9 %collective-permute-done.10 = bf16[1088,800]{0,1:T(8,128)(2,1)} collective-permute-done((bf16[1088,800]{0,1:T(8,128)(2,1)}, bf16[1088,800]{0,1:T(8,128)(2,1)}, u32[]{:S(2)}, u32[]{:S(2)}) %collective-permute-start.10) | collective-permute-done | bytes 1740832 | tf_op jit(solution)/shard_map/ppermute | solution.py:211
  330.8 2.9 bitcast_dynamic-update-slice_fusion
  333.7 7.2 %fusion.5.grad_ref = bf16[1088,512]{1,0:T(8,128)(2,1)S(1)} fusion(bf16[4,1088,800]{1,2,0:T(8,128)(2,1)} %bitcast_dynamic-update-slice_fusion, bf16[4,800,512]{2,1,0:T(8,128)(2,1)S(1)} %bitcast.142), kind=kOutput, calls=%fused_computation.10 | convolution fusion | flops 3565715456 | bytes 11354112 | tf_op jit(solution)/shard_map/ird,idc->rc/dot_general | solution.py:250
  340.9 33.6 %shard_map.85 = (bf16[1088,512]{1,0:T(8,128)(2,1)S(1)}, bf16[1088,1536]{1,0:T(8,128)(2,1)S(1)}) custom-call(s32[1]{0:T(128)} %dynamic_slice.60.length_ref, bf16[1088,1536]{1,0:T(8,128)(2,1)S(1)} %bitcast.125, bf16[1088,512]{1,0:T(8,128)(2,1)S(1)} %fusion.5.grad_ref), custom_call_target="tpu_custom_call" | custom-call | flops 8485076992 | bytes 8912896 | tf_op jit(solution)/shard_map/pallas_call | solution.py:149
  374.6 1.7 copy-done
  376.3 5.8 convolution_convert_fusion.2
  382.4 2.9 bitcast_dynamic-update-slice_fusion.5
  385.3 2.4 constant_dynamic-slice_fusion.4
  387.7 1.5 collective-permute-start
  389.5 2.2 bitcast_dynamic-update-slice_fusion.4
  391.7 1.5 collective-permute-start.1
  393.2 1.8 bitcast_dynamic-update-slice_fusion.3
  396.7 20.9 %collective-permute-done = bf16[1,400,1536]{2,1,0:T(8,128)(2,1)S(1)} collective-permute-done((bf16[1,400,1536]{2,1,0:T(8,128)(2,1)S(1)}, bf16[1,400,1536]{2,1,0:T(8,128)(2,1)S(1)}, u32[]{:S(2)}, u32[]{:S(2)}) %collective-permute-start) | collective-permute-done | bytes 1228832 | tf_op jit(solution)/shard_map/ppermute | solution.py:192
  419.8 24.1 %collective-permute-done.1 = bf16[1,400,1536]{2,1,0:T(8,128)(2,1)S(1)} collective-permute-done((bf16[1,400,1536]{2,1,0:T(8,128)(2,1)S(1)}, bf16[1,400,1536]{2,1,0:T(8,128)(2,1)S(1)}, u32[]{:S(2)}, u32[]{:S(2)}) %collective-permute-start.1) | collective-permute-done | bytes 1228832 | tf_op jit(solution)/shard_map/ppermute | solution.py:192
  446.2 23.6 %collective-permute-done.2 = bf16[1,400,1536]{2,1,0:T(8,128)(2,1)S(1)} collective-permute-done((bf16[1,400,1536]{2,1,0:T(8,128)(2,1)S(1)}, bf16[1,400,1536]{2,1,0:T(8,128)(2,1)S(1)}, u32[]{:S(2)}, u32[]{:S(2)}) %collective-permute-start.2) | collective-permute-done | bytes 1228832 | tf_op jit(solution)/shard_map/ppermute | solution.py:192
  471.0 14.8 %convolution_convert_fusion.1 = bf16[4,800,1536]{2,1,0:T(8,128)(2,1)} fusion(bf16[4,1088,800]{1,2,0:T(8,128)(2,1)S(1)} %bitcast_dynamic-update-slice_fusion.3, bf16[1088,1536]{1,0:T(8,128)(2,1)S(1)} %copy-done.1), kind=kOutput, calls=%fused_computation.1 | convolution fusion | flops 10700390400 | bytes 20135936 | tf_op jit(solution)/shard_map/ird,rc->idc/dot_general | solution.py:256
  485.9 15.6 %convolution_convert_fusion = bf16[4,800,1088]{2,1,0:T(8,128)(2,1)S(1)} fusion(bf16[4,800,1536]{2,1,0:T(8,128)(2,1)} %bitcast.8, bf16[1088,1536]{1,0:T(8,128)(2,1)S(1)} %copy-done.1), kind=kOutput, calls=%fused_computation | convolution fusion | flops 10698956800 | bytes 20135936 | tf_op jit(solution)/shard_map/rc,idc->ird/dot_general | solution.py:258
  502.4 3.3 collective-permute-done.19
  506.2 1.5 collective-permute-start.20
  508.3 40.2 %collective-permute-done.20 = bf16[1088,800]{0,1:T(8,128)(2,1)S(1)} collective-permute-done((bf16[1088,800]{0,1:T(8,128)(2,1)S(1)}, bf16[1088,800]{0,1:T(8,128)(2,1)S(1)}, u32[]{:S(2)}, u32[]{:S(2)}) %collective-permute-start.20) | collective-permute-done | bytes 1740832 | tf_op jit(solution)/shard_map/ppermute | solution.py:211
  549.2 2.4 copy.45
  551.5 11.9 %all-to-all-start.1 = ((bf16[4,272,800]{2,1,0:T(8,128)(2,1)}), bf16[4,272,800]{2,1,0:T(8,128)(2,1)S(1)}, u32[]{:S(2)}, u32[]{:S(2)}) async-start(bf16[4,272,800]{2,1,0:T(8,128)(2,1)} %bitcast.134), calls=%async_computation.1 | async-start | bytes 3899392 | tf_op jit(solution)/shard_map/all_to_all | solution.py:261
  563.4 2.5 bitcast_convert_fusion.1
  566.0 93.8 %all-to-all-done.1 = bf16[4,272,800]{2,1,0:T(8,128)(2,1)S(1)} async-done(((bf16[4,272,800]{2,1,0:T(8,128)(2,1)}), bf16[4,272,800]{2,1,0:T(8,128)(2,1)S(1)}, u32[]{:S(2)}, u32[]{:S(2)}) %all-to-all-start.1) | async-done | bytes 1740832 | tf_op jit(solution)/shard_map/all_to_all | solution.py:261
  659.8 2.0 copy.46
  661.8 33.5 %reduce-scatter.3.cloned.1.call-done = bf16[1,800,1536]{2,1,0:T(8,128)(2,1)} async-done(((bf16[4,800,1536]{2,1,0:T(8,128)(2,1)}), bf16[1,800,1536]{2,1,0:T(8,128)(2,1)}) %reduce-scatter.3.cloned.1.call-update) | async-done | bytes 2457616 | tf_op jit(solution)/shard_map/reduce_scatter | solution.py:257
  695.3 4.6 bitcast_convert_fusion
  (95 shorter events, 22.9 us)
Async XLA Ops:
  7.2 76.4 %all-gather.7.cloned.1.call-start = ((), (), s32[]{:S(2)}) async-start(), calls=%async_computation.7 | async-start | bytes 2048000 | tf_op jit(solution)/shard_map/all_gather | solution.py:187
  12.1 9.1 %copy-start.16 = (s32[4]{0:T(128)S(1)}, s32[4]{0:T(128)}, u32[]{:S(2)}) copy-start(s32[4]{0:T(128)} %param.11) | copy-start | bytes 52
  12.1 79.1 %all-to-all-start = ((bf16[4,272,800]{2,1,0:T(8,128)(2,1)}), bf16[4,272,800]{2,1,0:T(8,128)(2,1)S(1)}, u32[]{:S(2)}, u32[]{:S(2)}) async-start(bf16[4,272,800]{2,1,0:T(8,128)(2,1)} %bitcast.132), calls=%async_computation | async-start | bytes 3899392 | tf_op jit(solution)/shard_map/all_to_all | solution.py:179
  18.5 3.6 copy-start.14
  18.5 366.7 %all-gather.5.cloned.1.call-start = ((), (), s32[]{:S(2)}) async-start(), calls=%async_computation.6 | async-start | bytes 6144000 | tf_op jit(solution)/shard_map/all_gather | solution.py:187
  21.1 542.3 %reduce-scatter.5.cloned.1.call-start = ((), (), s32[]{:S(2)}) async-start(), calls=%async_computation.5 | async-start | bytes 4096000 | tf_op jit(solution)/shard_map/reduce_scatter | solution.py:255
  22.2 1.7 copy-start.11
  23.9 4.6 copy-start.9
  85.9 23.3 %collective-permute-start.15 = (bf16[1,400,512]{2,1,0:T(8,128)(2,1)}, bf16[1,400,512]{2,1,0:T(8,128)(2,1)}, u32[]{:S(2)}, u32[]{:S(2)}) collective-permute-start(bf16[1,400,512]{2,1,0:T(8,128)(2,1)} %get-tuple-element.36), channel_id=1, source_target_pairs={{0,16},{16,0},{1,17},{17,1},{2,18},{18,2},{3,19},{19,3},{4,20},{20... | collective-permute-start | bytes 1228808 | tf_op jit(solution)/shard_map/ppermute | solution.py:192
  87.4 162.4 %collective-permute-start.16 = (bf16[1,400,512]{2,1,0:T(8,128)(2,1)}, bf16[1,400,512]{2,1,0:T(8,128)(2,1)}, u32[]{:S(2)}, u32[]{:S(2)}) collective-permute-start(bf16[1,400,512]{2,1,0:T(8,128)(2,1)} %get-tuple-element.35), channel_id=1, source_target_pairs={{0,16},{16,0},{1,17},{17,1},{2,18},{18,2},{3,19},{19,3},{4,20},{20... | collective-permute-start | bytes 1228808 | tf_op jit(solution)/shard_map/ppermute | solution.py:192
  87.9 206.5 %collective-permute-start.17 = (bf16[1,400,512]{2,1,0:T(8,128)(2,1)}, bf16[1,400,512]{2,1,0:T(8,128)(2,1)}, u32[]{:S(2)}, u32[]{:S(2)}) collective-permute-start(bf16[1,400,512]{2,1,0:T(8,128)(2,1)} %get-tuple-element.34), channel_id=1, source_target_pairs={{0,16},{16,0},{1,17},{17,1},{2,18},{18,2},{3,19},{19,3},{4,20},{20... | collective-permute-start | bytes 1228808 | tf_op jit(solution)/shard_map/ppermute | solution.py:192
  91.2 3.6 copy-start.2
  96.3 73.0 %collective-permute-start.3 = (bf16[272,1536]{1,0:T(8,128)(2,1)}, bf16[272,1536]{1,0:T(8,128)(2,1)}, u32[]{:S(2)}, u32[]{:S(2)}) collective-permute-start(bf16[272,1536]{1,0:T(8,128)(2,1)} %get-tuple-element.30), channel_id=1, source_target_pairs={{0,1},{1,0},{2,3},{3,2},{4,5},{5,4},{6,7},{7,6},{8,9},{9,8},{10,11... | collective-permute-start | bytes 2506760 | tf_op jit(solution)/shard_map/ppermute | solution.py:205
  100.8 86.6 %collective-permute-start.4 = (bf16[272,1536]{1,0:T(8,128)(2,1)}, bf16[272,1536]{1,0:T(8,128)(2,1)}, u32[]{:S(2)}, u32[]{:S(2)}) collective-permute-start(bf16[272,1536]{1,0:T(8,128)(2,1)} %get-tuple-element.29), channel_id=1, source_target_pairs={{0,2},{1,3},{2,0},{3,1},{4,6},{5,7},{6,4},{7,5},{8,10},{9,11},{10,... | collective-permute-start | bytes 2506760 | tf_op jit(solution)/shard_map/ppermute | solution.py:205
  107.4 1.5 copy-start.8
  108.9 1.1 copy-start.15
  108.9 5.8 copy-start.10
  109.2 179.0 %copy-start.6 = (bf16[4,1088,800]{1,2,0:T(8,128)(2,1)}, bf16[4,1088,800]{1,2,0:T(8,128)(2,1)S(1)}, u32[]{:S(2)}) copy-start(bf16[4,1088,800]{1,2,0:T(8,128)(2,1)S(1)} %constant_dynamic-update-slice_fusion.1) | copy-start | bytes 20889604
  110.1 96.9 %copy-start.13 = (bf16[272,4,800]{2,1,0:T(4,128)(2,1)S(1)}, bf16[272,4,800]{2,1,0:T(4,128)(2,1)}, u32[]{:S(2)}) copy-start(bf16[272,4,800]{2,1,0:T(4,128)(2,1)} %param.6) | copy-start | bytes 5222404
  110.1 96.8 %collective-permute-start.5 = (bf16[272,1536]{1,0:T(8,128)(2,1)S(1)}, bf16[272,1536]{1,0:T(8,128)(2,1)S(1)}, u32[]{:S(2)}, u32[]{:S(2)}) collective-permute-start(bf16[272,1536]{1,0:T(8,128)(2,1)S(1)} %copy-done.15), channel_id=1, source_target_pairs={{0,3},{1,2},{2,1},{3,0},{4,7},{5,6},{6,5},{7,4},{8,11},{9,10},{10,... | collective-permute-start | bytes 2506760 | tf_op jit(solution)/shard_map/ppermute | solution.py:205
  169.4 133.2 %collective-permute-start.12 = (bf16[1088,800]{0,1:T(8,128)(2,1)}, bf16[1088,800]{0,1:T(8,128)(2,1)}, u32[]{:S(2)}, u32[]{:S(2)}) collective-permute-start(bf16[1088,800]{0,1:T(8,128)(2,1)} %copy.43), channel_id=1, source_target_pairs={{0,4},{4,0},{8,12},{12,8},{1,5},{5,1},{9,13},{13,9},{2,6},{6,2},{1... | collective-permute-start | bytes 5222408 | tf_op jit(solution)/shard_map/ppermute | solution.py:211
  187.4 107.1 %collective-permute-start.13 = (bf16[1088,800]{0,1:T(8,128)(2,1)}, bf16[1088,800]{0,1:T(8,128)(2,1)}, u32[]{:S(2)}, u32[]{:S(2)}) collective-permute-start(bf16[1088,800]{0,1:T(8,128)(2,1)} %copy.43), channel_id=1, source_target_pairs={{0,8},{4,12},{8,0},{12,4},{1,9},{5,13},{9,1},{13,5},{2,10},{6,14},... | collective-permute-start | bytes 5222408 | tf_op jit(solution)/shard_map/ppermute | solution.py:211
  207.3 60.0 %collective-permute-start.6 = (bf16[272,800]{1,0:T(8,128)(2,1)S(1)}, bf16[272,800]{1,0:T(8,128)(2,1)S(1)}, u32[]{:S(2)}, u32[]{:S(2)}) collective-permute-start(bf16[272,800]{1,0:T(8,128)(2,1)S(1)} %get-tuple-element.33), channel_id=1, source_target_pairs={{0,1},{1,0},{2,3},{3,2},{4,5},{5,4},{6,7},{7,6},{8,9},{9,8},{10,11... | collective-permute-start | bytes 1305608 | tf_op jit(solution)/shard_map/ppermute | solution.py:205
  251.6 35.9 %collective-permute-start.7 = (bf16[272,800]{1,0:T(8,128)(2,1)S(1)}, bf16[272,800]{1,0:T(8,128)(2,1)S(1)}, u32[]{:S(2)}, u32[]{:S(2)}) collective-permute-start(bf16[272,800]{1,0:T(8,128)(2,1)S(1)} %get-tuple-element.32), channel_id=1, source_target_pairs={{0,2},{1,3},{2,0},{3,1},{4,6},{5,7},{6,4},{7,5},{8,10},{9,11},{10,... | collective-permute-start | bytes 1305608 | tf_op jit(solution)/shard_map/ppermute | solution.py:205
  267.3 20.9 %collective-permute-start.8 = (bf16[272,800]{1,0:T(8,128)(2,1)S(1)}, bf16[272,800]{1,0:T(8,128)(2,1)S(1)}, u32[]{:S(2)}, u32[]{:S(2)}) collective-permute-start(bf16[272,800]{1,0:T(8,128)(2,1)S(1)} %get-tuple-element.31), channel_id=1, source_target_pairs={{0,3},{1,2},{2,1},{3,0},{4,7},{5,6},{6,5},{7,4},{8,11},{9,10},{10,... | collective-permute-start | bytes 1305608 | tf_op jit(solution)/shard_map/ppermute | solution.py:205
  293.0 37.8 %collective-permute-start.10 = (bf16[1088,800]{0,1:T(8,128)(2,1)}, bf16[1088,800]{0,1:T(8,128)(2,1)}, u32[]{:S(2)}, u32[]{:S(2)}) collective-permute-start(bf16[1088,800]{0,1:T(8,128)(2,1)} %copy.40), channel_id=1, source_target_pairs={{0,8},{4,12},{8,0},{12,4},{1,9},{5,13},{9,1},{13,5},{2,10},{6,14},... | collective-permute-start | bytes 5222408 | tf_op jit(solution)/shard_map/ppermute | solution.py:211
  294.5 36.3 %collective-permute-start.14 = (bf16[1088,800]{0,1:T(8,128)(2,1)}, bf16[1088,800]{0,1:T(8,128)(2,1)}, u32[]{:S(2)}, u32[]{:S(2)}) collective-permute-start(bf16[1088,800]{0,1:T(8,128)(2,1)} %collective-permute-done.13), channel_id=1, source_target_pairs={{0,4},{4,0},{8,12},{12,8},{1,5},{5,1},{9,13},{13,9},{2,6},{6,2},{1... | collective-permute-start | bytes 5222408 | tf_op jit(solution)/shard_map/ppermute | solution.py:211
  296.3 86.1 %collective-permute-start.9 = (bf16[1088,800]{0,1:T(8,128)(2,1)}, bf16[1088,800]{0,1:T(8,128)(2,1)}, u32[]{:S(2)}, u32[]{:S(2)}) collective-permute-start(bf16[1088,800]{0,1:T(8,128)(2,1)} %copy.40), channel_id=1, source_target_pairs={{0,4},{4,0},{8,12},{12,8},{1,5},{5,1},{9,13},{13,9},{2,6},{6,2},{1... | collective-permute-start | bytes 5222408 | tf_op jit(solution)/shard_map/ppermute | solution.py:211
  300.7 1.5 copy-start.7
  302.5 7.4 %copy-start.4 = (bf16[4,1088,800]{1,2,0:T(8,128)(2,1)}, bf16[4,1088,800]{1,2,0:T(8,128)(2,1)S(1)}, u32[]{:S(2)}) copy-start(bf16[4,1088,800]{1,2,0:T(8,128)(2,1)S(1)} %constant_dynamic-update-slice_fusion.2) | copy-start | bytes 20889604
  306.8 26.9 %copy-start.12 = (bf16[4,2,400,512]{3,2,1,0:T(8,128)(2,1)S(1)}, bf16[4,2,400,512]{3,2,1,0:T(8,128)(2,1)}, u32[]{:S(2)}) copy-start(bf16[4,2,400,512]{3,2,1,0:T(8,128)(2,1)} %bitcast_dynamic-update-slice_fusion.20) | copy-start | bytes 9830404
  330.8 62.4 %collective-permute-start.11 = (bf16[1088,800]{0,1:T(8,128)(2,1)}, bf16[1088,800]{0,1:T(8,128)(2,1)}, u32[]{:S(2)}, u32[]{:S(2)}) collective-permute-start(bf16[1088,800]{0,1:T(8,128)(2,1)} %collective-permute-done.10), channel_id=1, source_target_pairs={{0,4},{4,0},{8,12},{12,8},{1,5},{5,1},{9,13},{13,9},{2,6},{6,2},{1... | collective-permute-start | bytes 5222408 | tf_op jit(solution)/shard_map/ppermute | solution.py:211
  333.7 42.6 %slice-start = ((s8[7372800]{0:T(1024)(128)(4,1)}), s8[4194304]{0:T(1024)(128)(4,1)S(1)}, s32[]{:S(2)}) async-start(s8[7372800]{0:T(1024)(128)(4,1)} %bitcast.135), calls=%async_computation.8 | async-start | bytes 8388608
  340.9 35.4 %slice-start.1 = ((s8[7372800]{0:T(1024)(128)(4,1)}), s8[3178496]{0:T(1024)(128)(4,1)S(1)}, s32[]{:S(2)}) async-start(s8[7372800]{0:T(1024)(128)(4,1)} %bitcast.135), calls=%async_computation.9 | async-start | bytes 6356992
  374.6 1.7 copy-start
  382.1 313.2 %reduce-scatter.3.cloned.1.call-start = ((), (), s32[]{:S(2)}) async-start(), calls=%async_computation.4 | async-start | bytes 12288000 | tf_op jit(solution)/shard_map/reduce_scatter | solution.py:257
  385.3 4.2 copy-start.5
  387.7 7.9 %copy-start.3 = (bf16[1600,1536]{1,0:T(8,128)(2,1)S(1)}, bf16[1600,1536]{1,0:T(8,128)(2,1)}, u32[]{:S(2)}) copy-start(bf16[1600,1536]{1,0:T(8,128)(2,1)} %all-gather.5.cloned.1.call-done) | copy-start | bytes 14745604
  387.7 29.9 %collective-permute-start = (bf16[1,400,1536]{2,1,0:T(8,128)(2,1)S(1)}, bf16[1,400,1536]{2,1,0:T(8,128)(2,1)S(1)}, u32[]{:S(2)}, u32[]{:S(2)}) collective-permute-start(bf16[1,400,1536]{2,1,0:T(8,128)(2,1)S(1)} %get-tuple-element.27), channel_id=1, source_target_pairs={{0,16},{16,0},{1,17},{17,1},{2,18},{18,2},{3,19},{19,3},{4,20},{20... | collective-permute-start | bytes 3686408 | tf_op jit(solution)/shard_map/ppermute | solution.py:192
  391.7 52.3 %collective-permute-start.1 = (bf16[1,400,1536]{2,1,0:T(8,128)(2,1)S(1)}, bf16[1,400,1536]{2,1,0:T(8,128)(2,1)S(1)}, u32[]{:S(2)}, u32[]{:S(2)}) collective-permute-start(bf16[1,400,1536]{2,1,0:T(8,128)(2,1)S(1)} %get-tuple-element.26), channel_id=1, source_target_pairs={{0,16},{16,0},{1,17},{17,1},{2,18},{18,2},{3,19},{19,3},{4,20},{20... | collective-permute-start | bytes 3686408 | tf_op jit(solution)/shard_map/ppermute | solution.py:192
  395.0 74.9 %collective-permute-start.2 = (bf16[1,400,1536]{2,1,0:T(8,128)(2,1)S(1)}, bf16[1,400,1536]{2,1,0:T(8,128)(2,1)S(1)}, u32[]{:S(2)}, u32[]{:S(2)}) collective-permute-start(bf16[1,400,1536]{2,1,0:T(8,128)(2,1)S(1)} %get-tuple-element.25), channel_id=1, source_target_pairs={{0,16},{16,0},{1,17},{17,1},{2,18},{18,2},{3,19},{19,3},{4,20},{20... | collective-permute-start | bytes 3686408 | tf_op jit(solution)/shard_map/ppermute | solution.py:192
  419.8 51.2 %copy-start.1 = (bf16[1088,1536]{1,0:T(8,128)(2,1)S(1)}, bf16[1088,1536]{1,0:T(8,128)(2,1)}, u32[]{:S(2)}) copy-start(bf16[1088,1536]{1,0:T(8,128)(2,1)} %copy-done) | copy-start | bytes 10027012
  501.8 3.9 collective-permute-start.19
  501.9 6.4 collective-permute-start.18
  506.2 42.3 %collective-permute-start.20 = (bf16[1088,800]{0,1:T(8,128)(2,1)S(1)}, bf16[1088,800]{0,1:T(8,128)(2,1)S(1)}, u32[]{:S(2)}, u32[]{:S(2)}) collective-permute-start(bf16[1088,800]{0,1:T(8,128)(2,1)S(1)} %fusion), channel_id=1, source_target_pairs={{0,8},{4,12},{8,0},{12,4},{1,9},{5,13},{9,1},{13,5},{2,10},{6,14},... | collective-permute-start | bytes 5222408 | tf_op jit(solution)/shard_map/ppermute | solution.py:211
  551.5 108.3 %all-to-all-start.1 = ((bf16[4,272,800]{2,1,0:T(8,128)(2,1)}), bf16[4,272,800]{2,1,0:T(8,128)(2,1)S(1)}, u32[]{:S(2)}, u32[]{:S(2)}) async-start(bf16[4,272,800]{2,1,0:T(8,128)(2,1)} %bitcast.134), calls=%async_computation.1 | async-start | bytes 3899392 | tf_op jit(solution)/shard_map/all_to_all | solution.py:261
Sparse Core Ops, SparseCore 0:
  9.6 73.9 all-gather.6
  85.7 163.6 all-gather.4
  382.2 70.2 reduce-scatter.4
  486.0 209.2 reduce-scatter.2

commit v2 on v1

--- a/solution.py
+++ b/solution.py
@@ -182,17 +182,13 @@
 
 def weight_rows(weight):
     half = weight.shape[0] // 2
-    group, me = lax.axis_index("grp"), lax.axis_index("gy")
+    group = lax.axis_index("grp")
     share = lax.dynamic_slice_in_dim(weight, group * half, half, 0)
     mine = lax.all_gather(share, "gy")
-    full = jnp.zeros((4, 2) + share.shape, weight.dtype)
-    full = lax.dynamic_update_slice(full, weight.reshape((1, 2) + share.shape), (me, 0, 0, 0))
-    for bits in (1, 2, 3):
-        part = lax.dynamic_slice_in_dim(mine, me ^ bits, 1, 0)
-        other = lax.ppermute(part, "grp", [(0, 1), (1, 0)])
-        full = lax.dynamic_update_slice(full, part[None], (me ^ bits, group, 0, 0))
-        full = lax.dynamic_update_slice(full, other[None], (me ^ bits, 1 - group, 0, 0))
-    return full.reshape((4,) + weight.shape)
+    other = lax.ppermute(mine, "grp", [(0, 1), (1, 0)])
+    low = jnp.where(group == 0, mine, other)
+    high = jnp.where(group == 0, other, mine)
+    return jnp.concatenate([low, high], axis=1)
 
 
 def spread_images(rows):
@@ -242,11 +238,9 @@
     grad_rows = feature_blocks(grad_own)
     qkv, grad_own = lax.optimization_barrier((qkv, grad_own))
     qkv_rows = spread_images(qkv)
-    hidden, qkv_rows = lax.optimization_barrier((hidden, qkv_rows))
-    w_qkv, grad_own = lax.optimization_barrier((w_qkv, grad_own))
+    hidden, w_qkv, qkv_rows = lax.optimization_barrier((hidden, w_qkv, qkv_rows))
     w_qkv_full = weight_rows(w_qkv)
-    hidden_rows = feature_blocks(spread_images(hidden))
-    w_qkv_full, hidden_rows = lax.optimization_barrier((w_qkv_full, hidden_rows))
+    hidden_rows = feature_blocks(by_image(hidden))
     grad_attn = jnp.einsum(
         "ird,idc->rc", grad_rows, w_out_full, preferred_element_type=jnp.float32
     ).astype(jnp.bfloat16)

time: 714 us -> 626 us (0.88)
  starting transfers between devices: 80.8 us -> 47 us
  local copies, waits for them, and re-layouts: 94.8 us -> 61.1 us
  waiting for transfers between devices: 431 us -> 406 us
  other arithmetic: 8.37 us -> 16.9 us
    all_to_all x1 -> x2, waiting for transfers between devices: 0.01 us -> 65.2 us  [by_image(): swapped = lax.all_to_all(rows.transpose(1, 0, 2), 'gy', 0, 0)]
    all_gather x2, waiting for transfers between devices: 53.4 us -> 0.02 us  [weight_rows(): mine = lax.all_gather(share, 'gy')]
    all_to_all x1, waiting for transfers between devices: 93.8 us -> 42.3 us  [image_shards(): grad_hidden = lax.all_to_all(grad_hidden, 'gy', 0, 0).transpose(1, 0, 2)]
    ppermute x9, waiting for transfers between devices: 65 us -> 114 us  [flip(): return lax.ppermute(value, 'gx', [(i, i ^ bits) for i in range(4)])]
    ppermute x6 -> x3, starting transfers between devices: 49.4 us -> 4.45 us  [spread_images(): part = lax.ppermute(part, 'gy', [(i, i ^ bits) for i in range(4)])]
    ppermute x6 -> x3, waiting for transfers between devices: 117 us -> 77.1 us  [spread_images(): part = lax.ppermute(part, 'gy', [(i, i ^ bits) for i in range(4)])]
    ppermute x6 -> x2, waiting for transfers between devices: 68.6 us -> 107 us  [weight_rows(): other = lax.ppermute(mine, 'grp', [(0, 1), (1, 0)])]
    reduce_scatter x1, waiting for transfers between devices: 33.5 us -> 0.01 us  [image_shards(): grad_w_qkv = lax.psum_scatter(qkv_terms.astype(jnp.bfloat16), 'gy')]
  transfers between devices with their start and end apart: 27 -> 21, of which waited for: 15 -> 11; matrix products, arithmetic and copies ran while one was open for 19% -> 17% of each run, Pallas kernels for 5% -> 5%
where the time goes in v2:
time: 626 us; the launch traced here: 625 us
  waiting for transfers between devices  406 us (65%)
  local copies, waits for them, and re-layouts  61.1 us (10%)
  starting transfers between devices  47 us (8%)
  matrix products  46.7 us (7%)
  Pallas kernels  33.5 us (5%)
  other arithmetic  16.9 us (3%)
  between operations  14 us (2%)
    ppermute x9, waiting for transfers between devices, flip(): return lax.ppermute(value, 'gx', [(i, i ^ bits) for i in range(4)])  114 us
    ppermute x2, waiting for transfers between devices, weight_rows(): other = lax.ppermute(mine, 'grp', [(0, 1), (1, 0)])  107 us
    ppermute x3, waiting for transfers between devices, spread_images(): part = lax.ppermute(part, 'gy', [(i, i ^ bits) for i in range(4)])  77.1 us
    all_to_all x2, waiting for transfers between devices, by_image(): swapped = lax.all_to_all(rows.transpose(1, 0, 2), 'gy', 0, 0)  65.2 us
    all_to_all x1, waiting for transfers between devices, image_shards(): grad_hidden = lax.all_to_all(grad_hidden, 'gy', 0, 0).transpose(1, 0, 2)  42.3 us
    pallas_call x1, Pallas kernels, attention_backward(): pl.pallas_call(functools.partial(head_kernel, block), grid=(heads,), in_s...  33.5 us
    all_to_all x2, starting transfers between devices, by_image(): swapped = lax.all_to_all(rows.transpose(1, 0, 2), 'gy', 0, 0)  29.8 us
    dynamic_update_slice x8, local copies, waits for them, and re-layouts, feature_blocks(): full = lax.dynamic_update_index_in_dim(full, part, me ^ bits, 0)  15.8 us
  transfers between devices with their start and end apart: 21, of which 11 were waited for; matrix products, arithmetic and copies ran while one was open for 17% of the time, Pallas kernels for 5%

profile of v2, /device:TPU:0, one launch (start us, length us, event | category | flops | bytes accessed | tf_op | source)
XLA Modules:
  0.0 625.3 jit_solution(308698361101965075)
XLA Ops:
  7.2 3.2 copy.45
  10.4 6.3 %all-to-all-start = ((bf16[4,272,800]{2,1,0:T(8,128)(2,1)}), bf16[4,272,800]{2,1,0:T(8,128)(2,1)}, u32[]{:S(2)}, u32[]{:S(2)}) async-start(bf16[4,272,800]{2,1,0:T(8,128)(2,1)} %bitcast.85), calls=%async_computation | async-start | bytes 3899392 | tf_op jit(solution)/shard_map/all_to_all | solution.py:179
  16.7 45.1 %all-to-all-done = bf16[4,272,800]{2,1,0:T(8,128)(2,1)} async-done(((bf16[4,272,800]{2,1,0:T(8,128)(2,1)}), bf16[4,272,800]{2,1,0:T(8,128)(2,1)}, u32[]{:S(2)}, u32[]{:S(2)}) %all-to-all-start) | async-done | bytes 1740832 | tf_op jit(solution)/shard_map/all_to_all | solution.py:179
  61.8 2.6 copy.29
  64.4 1.7 copy-done.4
  66.1 1.5 dynamic-slice_bitcast_fusion.2
  67.6 1.8 constant_dynamic-slice_fusion
  69.5 2.1 collective-permute-start.1
  71.6 2.4 collective-permute-start.2
  74.0 0.3 broadcast_in_dim.39
  74.2 1.2 bitcast_dynamic-update-slice_fusion.9
  75.4 50.6 %collective-permute-done = bf16[272,1536]{1,0:T(8,128)(2,1)S(1)} collective-permute-done((bf16[272,1536]{1,0:T(8,128)(2,1)}, bf16[272,1536]{1,0:T(8,128)(2,1)S(1)}, u32[]{:S(2)}, u32[]{:S(2)}) %collective-permute-start) | collective-permute-done | bytes 835616 | tf_op jit(solution)/shard_map/ppermute | solution.py:201
  126.1 26.5 %collective-permute-done.1 = bf16[272,1536]{1,0:T(8,128)(2,1)} collective-permute-done((bf16[272,1536]{1,0:T(8,128)(2,1)}, bf16[272,1536]{1,0:T(8,128)(2,1)}, u32[]{:S(2)}, u32[]{:S(2)}) %collective-permute-start.1) | collective-permute-done | bytes 835616 | tf_op jit(solution)/shard_map/ppermute | solution.py:201
  152.7 1.2 bitcast_dynamic-update-slice_fusion.7
  154.0 1.7 copy-done.2
  155.7 1.1 constant_dynamic-slice_fusion.1
  156.8 3.9 copy.34
  160.8 1.5 collective-permute-start.5
  162.3 1.6 collective-permute-start.7
  163.9 0.7 dynamic_slice.31.length_ref
  164.5 2.8 copy.33
  167.3 28.8 %collective-permute-done.5 = bf16[1088,800]{0,1:T(8,128)(2,1)} collective-permute-done((bf16[1088,800]{0,1:T(8,128)(2,1)}, bf16[1088,800]{0,1:T(8,128)(2,1)}, u32[]{:S(2)}, u32[]{:S(2)}) %collective-permute-start.5) | collective-permute-done | bytes 1740832 | tf_op jit(solution)/shard_map/ppermute | solution.py:207
  196.1 3.4 broadcast.3.clone
  199.6 1.4 constant_dynamic-update-slice_fusion.1
  201.0 0.8 copy-done.6
  201.8 1.5 copy.44
  203.3 23.5 %all-to-all-start.2 = ((bf16[4,272,800]{2,1,0:T(8,128)(2,1)}), bf16[4,272,800]{2,1,0:T(8,128)(2,1)}, u32[]{:S(2)}, u32[]{:S(2)}) async-start(bf16[4,272,800]{2,1,0:T(8,128)(2,1)} %bitcast.82), calls=%async_computation.2 | async-start | bytes 3899392 | tf_op jit(solution)/shard_map/all_to_all | solution.py:179
  226.8 0.2 broadcast_select_fusion.3
  227.1 2.9 bitcast_dynamic-update-slice_fusion.5
  230.0 2.9 bitcast_dynamic-update-slice_fusion.4
  232.9 2.9 bitcast_dynamic-update-slice_fusion.3
  235.8 7.3 %fusion.15.grad_ref = bf16[1088,512]{1,0:T(8,128)(2,1)S(1)} fusion(bf16[4,1088,800]{1,2,0:T(8,128)(2,1)} %bitcast_dynamic-update-slice_fusion.3, bf16[4,400,512]{2,1,0:T(8,128)(2,1)S(1)} %get-tuple-element.29, bf16[4,400,512]{2,1,0:T(8,128)(2,1)S(1)} %get-tuple-element.28), kind=kOutput, calls=%fused_computation.19 | convolution fusion | flops 3572269056 | bytes 11354112 | tf_op jit(solution)/shard_map/ird,idc->rc/dot_general | solution.py:244
  243.1 33.5 %shard_map.85 = (bf16[1088,512]{1,0:T(8,128)(2,1)S(1)}, bf16[1088,1536]{1,0:T(8,128)(2,1)S(1)}) custom-call(s32[1]{0:T(128)} %dynamic_slice.31.length_ref, bf16[1088,1536]{1,0:T(8,128)(2,1)S(1)} %bitcast.84, bf16[1088,512]{1,0:T(8,128)(2,1)S(1)} %fusion.15.grad_ref), custom_call_target="tpu_custom_call" | custom-call | flops 8485076992 | bytes 8912896 | tf_op jit(solution)/shard_map/pallas_call | solution.py:149
  276.6 8.9 %convolution_convert_fusion.2 = bf16[4,800,512]{2,1,0:T(8,128)(2,1)} fusion(bf16[4,1088,800]{1,2,0:T(8,128)(2,1)} %bitcast_dynamic-update-slice_fusion.3, bf16[1088,512]{1,0:T(8,128)(2,1)S(1)} %get-tuple-element.14), kind=kOutput, calls=%fused_computation.21 | convolution fusion | flops 3566796800 | bytes 11354112 | tf_op jit(solution)/shard_map/ird,rc->idc/dot_general | solution.py:248
  285.6 20.0 %all-to-all-done.2 = bf16[4,272,800]{2,1,0:T(8,128)(2,1)} async-done(((bf16[4,272,800]{2,1,0:T(8,128)(2,1)}), bf16[4,272,800]{2,1,0:T(8,128)(2,1)}, u32[]{:S(2)}, u32[]{:S(2)}) %all-to-all-start.2) | async-done | bytes 1740832 | tf_op jit(solution)/shard_map/all_to_all | solution.py:179
  305.7 4.0 copy.39
  309.6 1.4 collective-permute-start.12
  311.1 41.1 %collective-permute-done.12 = bf16[1088,800]{0,1:T(8,128)(2,1)} collective-permute-done((bf16[1088,800]{0,1:T(8,128)(2,1)}, bf16[1088,800]{0,1:T(8,128)(2,1)}, u32[]{:S(2)}, u32[]{:S(2)}) %collective-permute-start.12) | collective-permute-done | bytes 1740832 | tf_op jit(solution)/shard_map/ppermute | solution.py:207
  352.2 3.9 copy.38
  356.1 0.5 broadcast.3.clone.1
  356.6 1.0 copy-done.5
  357.6 0.3 constant_dynamic-update-slice_fusion
  357.8 1.8 bitcast_dynamic-update-slice_fusion.2
  359.6 1.8 bitcast_dynamic-update-slice_fusion.1
  361.4 1.8 bitcast_dynamic-update-slice_fusion
  363.2 14.8 %convolution_convert_fusion.1 = bf16[4,800,1536]{2,1,0:T(8,128)(2,1)} fusion(bf16[4,1088,800]{1,2,0:T(8,128)(2,1)S(1)} %bitcast_dynamic-update-slice_fusion, bf16[1088,1536]{1,0:T(8,128)(2,1)S(1)} %get-tuple-element.12), kind=kOutput, calls=%fused_computation.1 | convolution fusion | flops 10700390400 | bytes 20135936 | tf_op jit(solution)/shard_map/ird,rc->idc/dot_general | solution.py:250
  378.1 1.5 collective-permute-start.3
  379.6 107.4 %collective-permute-done.3 = bf16[4,400,1536]{2,1,0:T(8,128)(2,1)} collective-permute-done((bf16[4,400,1536]{2,1,0:T(8,128)(2,1)}, bf16[4,400,1536]{2,1,0:T(8,128)(2,1)}, u32[]{:S(2)}, u32[]{:S(2)}) %collective-permute-start.3) | collective-permute-done | bytes 4915232 | tf_op jit(solution)/shard_map/ppermute | solution.py:188
  487.0 8.3 %broadcast_select_fusion.1 = (bf16[4,400,1536]{2,1,0:T(8,128)(2,1)}, bf16[4,400,1536]{2,1,0:T(8,128)(2,1)}) fusion(bf16[4,400,1536]{2,1,0:T(8,128)(2,1)} %bitcast.87, bf16[4,400,1536]{2,1,0:T(8,128)(2,1)} %collective-permute-done.3, pred[]{:T(512)S(6)} %eq.2), kind=kLoop, calls=%fused_computation.6 | loop fusion | flops 4915200 | bytes 19660800 | tf_op jit(solution)/shard_map/jit(_where)/select_n | solution.py:189
  495.3 15.7 %convolution_convert_fusion = bf16[4,800,1088]{2,1,0:T(8,128)(2,1)S(1)} fusion(bf16[4,400,1536]{2,1,0:T(8,128)(2,1)} %get-tuple-element.22, bf16[4,400,1536]{2,1,0:T(8,128)(2,1)} %get-tuple-element.21, bf16[1088,1536]{1,0:T(8,128)(2,1)S(1)} %get-tuple-element.12), kind=kOutput, calls=%fused_computation | convolution fusion | flops 10718617600 | bytes 20135936 | tf_op jit(solution)/shard_map/rc,idc->ird/dot_general | solution.py:252
  511.0 0.3 dynamic-slice_bitcast_fusion.1
  511.4 0.5 collective-permute-start.8
  511.9 3.3 collective-permute-done.9
  515.2 0.5 fusion.3
  515.7 1.5 collective-permute-start.10
  517.2 0.6 collective-permute-done.8
  517.8 40.2 %collective-permute-done.10 = bf16[1088,800]{0,1:T(8,128)(2,1)S(1)} collective-permute-done((bf16[1088,800]{0,1:T(8,128)(2,1)S(1)}, bf16[1088,800]{0,1:T(8,128)(2,1)S(1)}, u32[]{:S(2)}, u32[]{:S(2)}) %collective-permute-start.10) | collective-permute-done | bytes 1740832 | tf_op jit(solution)/shard_map/ppermute | solution.py:207
  558.0 0.7 fusion.5
  558.7 2.4 copy.36
  561.0 4.4 all-to-all-start.1
  565.5 2.5 bitcast_convert_fusion.1
  568.1 42.3 %all-to-all-done.1 = bf16[4,272,800]{2,1,0:T(8,128)(2,1)} async-done(((bf16[4,272,800]{2,1,0:T(8,128)(2,1)}), bf16[4,272,800]{2,1,0:T(8,128)(2,1)}, u32[]{:S(2)}, u32[]{:S(2)}) %all-to-all-start.1) | async-done | bytes 1740832 | tf_op jit(solution)/shard_map/all_to_all | solution.py:255
  610.4 3.7 copy.41
  614.1 4.6 bitcast_convert_fusion
  (40 shorter events, 0.5 us)
Async XLA Ops:
  7.2 148.5 %copy-start = (bf16[800,1536]{1,0:T(8,128)(2,1)S(1)}, bf16[800,1536]{1,0:T(8,128)(2,1)}, u32[]{:S(2)}) copy-start(bf16[800,1536]{1,0:T(8,128)(2,1)} %param.8) | copy-start | bytes 7372804
  10.4 51.5 %all-to-all-start = ((bf16[4,272,800]{2,1,0:T(8,128)(2,1)}), bf16[4,272,800]{2,1,0:T(8,128)(2,1)}, u32[]{:S(2)}, u32[]{:S(2)}) async-start(bf16[4,272,800]{2,1,0:T(8,128)(2,1)} %bitcast.85), calls=%async_computation | async-start | bytes 3899392 | tf_op jit(solution)/shard_map/all_to_all | solution.py:179
  16.7 145.6 %all-gather.7.cloned.1.call-start = ((), (), s32[]{:S(2)}) async-start(), calls=%async_computation.8 | async-start | bytes 2048000 | tf_op jit(solution)/shard_map/all_gather | solution.py:187
  64.4 1.7 copy-start.4
  67.6 58.4 %collective-permute-start = (bf16[272,1536]{1,0:T(8,128)(2,1)}, bf16[272,1536]{1,0:T(8,128)(2,1)S(1)}, u32[]{:S(2)}, u32[]{:S(2)}) collective-permute-start(bf16[272,1536]{1,0:T(8,128)(2,1)} %get-tuple-element.27), channel_id=1, source_target_pairs={{0,1},{1,0},{2,3},{3,2},{4,5},{5,4},{6,7},{7,6},{8,9},{9,8},{10,11... | collective-permute-start | bytes 2506760 | tf_op jit(solution)/shard_map/ppermute | solution.py:201
  69.5 308.6 %all-gather.5.cloned.1.call-start = ((), (), s32[]{:S(2)}) async-start(), calls=%async_computation.7 | async-start | bytes 6144000 | tf_op jit(solution)/shard_map/all_gather | solution.py:187
  69.5 83.1 %collective-permute-start.1 = (bf16[272,1536]{1,0:T(8,128)(2,1)}, bf16[272,1536]{1,0:T(8,128)(2,1)}, u32[]{:S(2)}, u32[]{:S(2)}) collective-permute-start(bf16[272,1536]{1,0:T(8,128)(2,1)} %get-tuple-element.26), channel_id=1, source_target_pairs={{0,2},{1,3},{2,0},{3,1},{4,6},{5,7},{6,4},{7,5},{8,10},{9,11},{10,... | collective-permute-start | bytes 2506760 | tf_op jit(solution)/shard_map/ppermute | solution.py:201
  71.6 82.3 %collective-permute-start.2 = (bf16[272,1536]{1,0:T(8,128)(2,1)}, bf16[272,1536]{1,0:T(8,128)(2,1)S(1)}, u32[]{:S(2)}, u32[]{:S(2)}) collective-permute-start(bf16[272,1536]{1,0:T(8,128)(2,1)} %get-tuple-element.25), channel_id=1, source_target_pairs={{0,3},{1,2},{2,1},{3,0},{4,7},{5,6},{6,5},{7,4},{8,11},{9,10},{10,... | collective-permute-start | bytes 2506760 | tf_op jit(solution)/shard_map/ppermute | solution.py:201
  154.0 1.7 copy-start.2
  155.7 8.2 %copy-start.8 = (s32[4]{0:T(128)S(1)}, s32[4]{0:T(128)}, u32[]{:S(2)}) copy-start(s32[4]{0:T(128)} %param.11) | copy-start | bytes 52
  160.8 35.4 %collective-permute-start.5 = (bf16[1088,800]{0,1:T(8,128)(2,1)}, bf16[1088,800]{0,1:T(8,128)(2,1)}, u32[]{:S(2)}, u32[]{:S(2)}) collective-permute-start(bf16[1088,800]{0,1:T(8,128)(2,1)} %copy.34), channel_id=1, source_target_pairs={{0,8},{4,12},{8,0},{12,4},{1,9},{5,13},{9,1},{13,5},{2,10},{6,14},... | collective-permute-start | bytes 5222408 | tf_op jit(solution)/shard_map/ppermute | solution.py:207
  162.3 64.6 %collective-permute-start.7 = (bf16[4,400,512]{2,1,0:T(8,128)(2,1)}, bf16[4,400,512]{2,1,0:T(8,128)(2,1)S(1)}, u32[]{:S(2)}, u32[]{:S(2)}) collective-permute-start(bf16[4,400,512]{2,1,0:T(8,128)(2,1)} %bitcast.88), channel_id=1, source_target_pairs={{0,16},{16,0},{1,17},{17,1},{2,18},{18,2},{3,19},{19,3},{4,20},{20... | collective-permute-start | bytes 4915208 | tf_op jit(solution)/shard_map/ppermute | solution.py:188
  163.8 63.2 %collective-permute-start.4 = (bf16[1088,800]{0,1:T(8,128)(2,1)}, bf16[1088,800]{0,1:T(8,128)(2,1)}, u32[]{:S(2)}, u32[]{:S(2)}) collective-permute-start(bf16[1088,800]{0,1:T(8,128)(2,1)} %copy.34), channel_id=1, source_target_pairs={{0,4},{4,0},{8,12},{12,8},{1,5},{5,1},{9,13},{13,9},{2,6},{6,2},{1... | collective-permute-start | bytes 5222408 | tf_op jit(solution)/shard_map/ppermute | solution.py:207
  196.1 36.7 %collective-permute-start.6 = (bf16[1088,800]{0,1:T(8,128)(2,1)}, bf16[1088,800]{0,1:T(8,128)(2,1)}, u32[]{:S(2)}, u32[]{:S(2)}) collective-permute-start(bf16[1088,800]{0,1:T(8,128)(2,1)} %collective-permute-done.5), channel_id=1, source_target_pairs={{0,4},{4,0},{8,12},{12,8},{1,5},{5,1},{9,13},{13,9},{2,6},{6,2},{1... | collective-permute-start | bytes 5222408 | tf_op jit(solution)/shard_map/ppermute | solution.py:207
  199.6 2.2 copy-start.6
  201.8 25.0 %copy-start.7 = (bf16[1600,512]{1,0:T(8,128)(2,1)S(1)}, bf16[1600,512]{1,0:T(8,128)(2,1)}, u32[]{:S(2)}) copy-start(bf16[1600,512]{1,0:T(8,128)(2,1)} %all-gather.7.cloned.1.call-done) | copy-start | bytes 4915204
  203.3 102.4 %all-to-all-start.2 = ((bf16[4,272,800]{2,1,0:T(8,128)(2,1)}), bf16[4,272,800]{2,1,0:T(8,128)(2,1)}, u32[]{:S(2)}, u32[]{:S(2)}) async-start(bf16[4,272,800]{2,1,0:T(8,128)(2,1)} %bitcast.82), calls=%async_computation.2 | async-start | bytes 3899392 | tf_op jit(solution)/shard_map/all_to_all | solution.py:179
  226.8 338.7 %reduce-scatter.5.cloned.1.call-start = ((), (), s32[]{:S(2)}) async-start(), calls=%async_computation.6 | async-start | bytes 4096000 | tf_op jit(solution)/shard_map/reduce_scatter | solution.py:249
  235.8 7.3 %copy-start.3 = (bf16[4,272,1536]{2,1,0:T(8,128)(2,1)S(1)}, bf16[4,272,1536]{2,1,0:T(8,128)(2,1)}, u32[]{:S(2)}) copy-start(bf16[4,272,1536]{2,1,0:T(8,128)(2,1)} %copy-done.2) | copy-start | bytes 10027012
  285.6 328.5 %reduce-scatter.3.cloned.1.call-start = ((), (), s32[]{:S(2)}) async-start(), calls=%async_computation.5 | async-start | bytes 12288000 | tf_op jit(solution)/shard_map/reduce_scatter | solution.py:251
  309.6 42.5 %collective-permute-start.12 = (bf16[1088,800]{0,1:T(8,128)(2,1)}, bf16[1088,800]{0,1:T(8,128)(2,1)}, u32[]{:S(2)}, u32[]{:S(2)}) collective-permute-start(bf16[1088,800]{0,1:T(8,128)(2,1)} %copy.39), channel_id=1, source_target_pairs={{0,8},{4,12},{8,0},{12,4},{1,9},{5,13},{9,1},{13,5},{2,10},{6,14},... | collective-permute-start | bytes 5222408 | tf_op jit(solution)/shard_map/ppermute | solution.py:207
  311.1 46.8 %collective-permute-start.11 = (bf16[1088,800]{0,1:T(8,128)(2,1)}, bf16[1088,800]{0,1:T(8,128)(2,1)}, u32[]{:S(2)}, u32[]{:S(2)}) collective-permute-start(bf16[1088,800]{0,1:T(8,128)(2,1)} %copy.39), channel_id=1, source_target_pairs={{0,4},{4,0},{8,12},{12,8},{1,5},{5,1},{9,13},{13,9},{2,6},{6,2},{1... | collective-permute-start | bytes 5222408 | tf_op jit(solution)/shard_map/ppermute | solution.py:207
  352.2 9.3 %collective-permute-start.13 = (bf16[1088,800]{0,1:T(8,128)(2,1)}, bf16[1088,800]{0,1:T(8,128)(2,1)}, u32[]{:S(2)}, u32[]{:S(2)}) collective-permute-start(bf16[1088,800]{0,1:T(8,128)(2,1)} %collective-permute-done.12), channel_id=1, source_target_pairs={{0,4},{4,0},{8,12},{12,8},{1,5},{5,1},{9,13},{13,9},{2,6},{6,2},{1... | collective-permute-start | bytes 5222408 | tf_op jit(solution)/shard_map/ppermute | solution.py:207
  356.1 1.5 copy-start.5
  378.1 108.9 %collective-permute-start.3 = (bf16[4,400,1536]{2,1,0:T(8,128)(2,1)}, bf16[4,400,1536]{2,1,0:T(8,128)(2,1)}, u32[]{:S(2)}, u32[]{:S(2)}) collective-permute-start(bf16[4,400,1536]{2,1,0:T(8,128)(2,1)} %bitcast.86), channel_id=1, source_target_pairs={{0,16},{16,0},{1,17},{17,1},{2,18},{18,2},{3,19},{19,3},{4,20},{20... | collective-permute-start | bytes 14745608 | tf_op jit(solution)/shard_map/ppermute | solution.py:188
  511.3 3.9 collective-permute-start.9
  511.4 6.4 %collective-permute-start.8 = (bf16[1088,800]{0,1:T(8,128)(2,1)S(1)}, bf16[1088,800]{0,1:T(8,128)(2,1)S(1)}, u32[]{:S(2)}, u32[]{:S(2)}) collective-permute-start(bf16[1088,800]{0,1:T(8,128)(2,1)S(1)} %get-tuple-element.23), channel_id=1, source_target_pairs={{0,4},{4,0},{8,12},{12,8},{1,5},{5,1},{9,13},{13,9},{2,6},{6,2},{1... | collective-permute-start | bytes 5222408 | tf_op jit(solution)/shard_map/ppermute | solution.py:207
  515.7 42.3 %collective-permute-start.10 = (bf16[1088,800]{0,1:T(8,128)(2,1)S(1)}, bf16[1088,800]{0,1:T(8,128)(2,1)S(1)}, u32[]{:S(2)}, u32[]{:S(2)}) collective-permute-start(bf16[1088,800]{0,1:T(8,128)(2,1)S(1)} %fusion.3), channel_id=1, source_target_pairs={{0,8},{4,12},{8,0},{12,4},{1,9},{5,13},{9,1},{13,5},{2,10},{6,14},... | collective-permute-start | bytes 5222408 | tf_op jit(solution)/shard_map/ppermute | solution.py:207
  561.0 49.4 %all-to-all-start.1 = ((bf16[4,272,800]{2,1,0:T(8,128)(2,1)}), bf16[4,272,800]{2,1,0:T(8,128)(2,1)}, u32[]{:S(2)}, u32[]{:S(2)}) async-start(bf16[4,272,800]{2,1,0:T(8,128)(2,1)} %bitcast.26), calls=%async_computation.1 | async-start | bytes 3899392 | tf_op jit(solution)/shard_map/all_to_all | solution.py:255
  610.4 8.3 %copy-start.1 = (bf16[800,1536]{1,0:T(8,128)(2,1)S(1)}, bf16[800,1536]{1,0:T(8,128)(2,1)}, u32[]{:S(2)}) copy-start(bf16[800,1536]{1,0:T(8,128)(2,1)} %param.8) | copy-start | bytes 7372804
Sparse Core Ops, SparseCore 0:
  69.6 86.8 all-gather.6
  158.7 142.6 all-gather.4
  303.6 60.4 reduce-scatter.4
  378.2 165.8 reduce-scatter.2
